TPU v7x, 32 devices: a whole 2x2x4 slice. The times are simulated.
32 devices in a mesh: row: 8 (over y, x, core), col: 4 (over z).
Axes of the slice: x: 2, y: 2, z: 4, core: 2. Of those that a mesh axis runs over, the one named last changes fastest.
Arguments:
- stem: bfloat16 [8, 4, 1, 512, 2, 512], P('row', 'col'), may hold values from -6 to 6
- branch: bfloat16 [8, 4, 2, 512, 512], P('row', None, None, None, 'col'), may hold values from -0.1875 to 0.1875
Outputs:
- amplitudes: bfloat16 [8, 4, 1, 512, 2, 512], P('row', 'col')
All inputs are finite; a program needn't handle non-finite values.
Results may differ from a plain program's by a relative error of at most 0.0075.
Values may be sent and summed in bfloat16 or wider, within the bound.
A program may use at most 64 MiB of HBM per device.

v0:
```python
import jax
import jax.numpy as jnp
from jax import lax
from jax.sharding import PartitionSpec as P


def right_piece(block, piece):
    width = piece.shape[2]
    items = block.shape[0]
    order_size = block.shape[1]
    flat = block.reshape(items * order_size, 2 * width)
    real_t = piece[0].T
    imag_t = piece[1].T
    weight = jnp.block([[real_t, imag_t], [-imag_t, real_t]])
    product = jnp.dot(flat, weight, preferred_element_type=jnp.float32)
    return product.reshape(items, order_size, 2, order_size)


def left_piece(block, piece):
    rows_out = piece.shape[1]
    real_in = block[:, :, 0, :]
    imag_in = block[:, :, 1, :]
    real_w = piece[0]
    imag_w = piece[1]
    weight_real = jnp.concatenate([real_w, imag_w], axis=0)
    weight_imag = jnp.concatenate([-imag_w, real_w], axis=0)
    product = jnp.einsum("xi,eij->exj", weight_real, real_in, preferred_element_type=jnp.float32)
    product = product + jnp.einsum(
        "xi,eij->exj", weight_imag, imag_in, preferred_element_type=jnp.float32
    )
    return jnp.stack([product[:, :rows_out, :], product[:, rows_out:, :]], axis=2)


def shards(stem, branch):
    slab_count = stem.shape[2]
    order_size = stem.shape[3]
    row_count = lax.axis_size("row")
    share = order_size // row_count
    own_columns = branch[0]
    whole = lax.all_gather(own_columns, "col", axis=3, tiled=True)

    def apply_right(block, build_id):
        return right_piece(block, whole[build_id])

    def apply_left(block, build_id):
        return left_piece(block, whole[build_id])

    block = stem[0, 0]
    half_first = apply_right(block, 1).astype(jnp.bfloat16)
    step_first = apply_left(half_first, 0).astype(jnp.bfloat16)
    outgoing = step_first.reshape(slab_count, row_count, share, 2, order_size)
    moved = lax.all_to_all(outgoing, "row", split_axis=1, concat_axis=1, tiled=True)
    items = moved.shape[0]
    flat = moved.reshape(items, order_size, 2, order_size)
    half_second = apply_right(flat, 3).astype(jnp.bfloat16)
    step_second = apply_left(half_second, 2).astype(jnp.bfloat16)
    leaving = step_second.reshape(slab_count, order_size, 2, row_count, share)
    arrived = lax.all_to_all(leaving, "row", split_axis=3, concat_axis=3, tiled=True)
    return arrived.reshape(1, 1, slab_count, order_size, 2, order_size)


def solution(mesh):
    placed = (P("row", "col", None, None, None, None), P("row", None, None, None, "col"))
    return jax.shard_map(
        shards,
        mesh=mesh,
        in_specs=placed,
        out_specs=P("row", "col", None, None, None, None),
        check_vma=False,
    )
```

profile of v0, /device:TPU:0, one launch (start us, length us, event | category | flops | bytes accessed | tf_op | source)
XLA Modules:
  0.0 157.7 jit_solution(13358634369063110201)
XLA Ops:
  6.5 0.0 all-gather.3.cloned.1.call-start
  6.5 0.7 all-gather.3.cloned.1.call-update
  7.3 1.5 copy.17
  8.7 83.5 %all-gather.3.cloned.1.call-done = bf16[1,4,2,512,512]{4,3,2,1,0:T(8,128)(2,1)} async-done(((bf16[1,4,2,512,128]{4,3,2,1,0:T(8,128)(2,1)}), bf16[1,4,2,512,512]{4,3,2,1,0:T(8,128)(2,1)}) %all-gather.3.cloned.1.call-update) | async-done | bytes 4194320 | tf_op jit(solution)/shard_map/all_gather | solution.py:40
  92.2 0.0 copy-start
  92.2 2.2 %fusion.36 = (bf16[512,512]{1,0:T(8,128)(2,1)}, bf16[512,512]{1,0:T(8,128)(2,1)S(1)}) fusion(bf16[4,2,512,512]{3,2,1,0:T(8,128)(2,1)} %bitcast.76), kind=kLoop, calls=%fused_computation.52 | loop fusion | flops 524288 | bytes 2097152 | tf_op jit(solution)/shard_map/neg | solution.py:26
  94.4 2.1 %fusion.35 = (bf16[512,512]{0,1:T(8,128)(2,1)}, bf16[512,512]{0,1:T(8,128)(2,1)S(1)}) fusion(bf16[4,2,512,512]{3,2,1,0:T(8,128)(2,1)} %bitcast.77), kind=kLoop, calls=%fused_computation.51 | loop fusion | flops 524288 | bytes 2097152 | tf_op jit(solution)/shard_map/neg | solution.py:14
  96.5 0.0 copy-done
  96.5 0.4 slice_bitcast_fusion.6
  96.9 1.3 fusion.8
  98.2 0.7 fusion.14
  99.0 0.8 fusion.12
  99.7 0.9 fusion.38
  100.6 1.3 copy.9
  101.9 1.0 copy.10
  102.9 1.1 pad_maximum_fusion
  104.0 1.1 copy.11
  105.1 3.7 %all-to-all-start = ((bf16[1,8,64,2,512]{4,2,3,0,1:T(8,128)(2,1)}), bf16[1,8,64,2,512]{4,2,3,0,1:T(8,128)(2,1)S(1)}, u32[]{:S(2)}, u32[]{:S(2)}) async-start(bf16[1,8,64,2,512]{4,2,3,0,1:T(8,128)(2,1)} %copy.11), calls=%async_computation | async-start | bytes 2097152 | tf_op jit(solution)/shard_map/all_to_all | solution.py:52
  108.7 2.7 %maximum_maximum_fusion = bf16[1024,1024]{0,1:T(8,128)(2,1)} fusion(bf16[512,512]{0,1:T(8,128)(2,1)S(1)} %get-tuple-element.10, bf16[512,512]{0,1:T(8,128)(2,1)} %get-tuple-element.15, bf16[512,512]{0,1:T(8,128)(2,1)S(1)} %get-tuple-element.7), kind=kLoop, calls=%fused_computation.8 | loop fusion | flops 8388608 | bytes 3670016 | tf_op jit(solution)/shard_map/jit(block)/concatenate | solution.py:14
  111.4 12.7 %all-to-all-done = bf16[1,8,64,2,512]{4,2,3,0,1:T(8,128)(2,1)S(1)} async-done(((bf16[1,8,64,2,512]{4,2,3,0,1:T(8,128)(2,1)}), bf16[1,8,64,2,512]{4,2,3,0,1:T(8,128)(2,1)S(1)}, u32[]{:S(2)}, u32[]{:S(2)}) %all-to-all-start) | async-done | bytes 1048608 | tf_op jit(solution)/shard_map/all_to_all | solution.py:52
  124.1 1.1 copy.12
  125.2 0.8 reshape.153
  126.0 2.9 %fusion.11 = bf16[1,512,2,512]{3,1,2,0:T(8,128)(2,1)S(1)} fusion(bf16[512,1024,1]{1,0,2:T(8,128)(2,1)S(1)} %reshape.153, bf16[2,512,1024]{2,1,0:T(8,128)(2,1)} %bitcast.80), kind=kOutput, calls=%fused_computation.13 | convolution fusion | flops 1074266112 | bytes 4194304 | tf_op jit(solution)/shard_map/dot_general | solution.py:15
  128.9 0.0 copy-start.1
  128.9 0.8 fusion.21
  129.6 0.3 copy-done.1
  129.9 0.8 fusion.13
  130.7 0.1 fusion.37
  130.8 0.1 pad_maximum_fusion.1
  130.9 17.8 %all_to_all.10 = bf16[1,512,2,8,64]{1,4,2,0,3:T(8,128)(2,1)S(1)} all-to-all(bf16[1,512,2,8,64]{1,4,2,0,3:T(8,128)(2,1)S(1)} %pad_maximum_fusion.1), channel_id=1, replica_groups=mesh['row'=8,'col'=4] {'row'}, dimensions={3} | all-to-all | bytes 2097152 | tf_op jit(solution)/shard_map/all_to_all | solution.py:58
  148.7 0.1 copy.15
  148.8 2.1 %copy.16 = bf16[1,1,1,512,2,512]{5,4,3,2,1,0:T(2,128)(2,1)} copy(bf16[1,1,1,512,2,512]{3,5,4,2,1,0:T(8,128)(2,1)S(1)} %bitcast.79) | data formatting | bytes 2097152 | tf_op jit(solution)/shard_map/reshape | solution.py:59
Async XLA Ops:
  6.5 85.7 %all-gather.3.cloned.1.call-start = ((), (), s32[]{:S(2)}) async-start(), calls=%async_computation.2 | async-start | bytes 5242880 | tf_op jit(solution)/shard_map/all_gather | solution.py:40
  92.2 4.3 %copy-start = (bf16[1,4,2,512,512]{4,3,2,1,0:T(8,128)(2,1)S(1)}, bf16[1,4,2,512,512]{4,3,2,1,0:T(8,128)(2,1)}, u32[]{:S(2)}) copy-start(bf16[1,4,2,512,512]{4,3,2,1,0:T(8,128)(2,1)} %all-gather.3.cloned.1.call-done) | copy-start | bytes 12582916
  105.1 19.1 %all-to-all-start = ((bf16[1,8,64,2,512]{4,2,3,0,1:T(8,128)(2,1)}), bf16[1,8,64,2,512]{4,2,3,0,1:T(8,128)(2,1)S(1)}, u32[]{:S(2)}, u32[]{:S(2)}) async-start(bf16[1,8,64,2,512]{4,2,3,0,1:T(8,128)(2,1)} %copy.11), calls=%async_computation | async-start | bytes 2097152 | tf_op jit(solution)/shard_map/all_to_all | solution.py:52
  128.9 1.0 copy-start.1
Sparse Core Ops, SparseCore 0:
  8.9 83.2 all-gather.2
where the time goes:
time: 158 us
  waiting for transfers between devices  96.9 us (61%)
  blocking collectives  17.8 us (11%)
  between operations  13.5 us (9%)
  local copies, waits for them, and re-layouts  10.5 us (7%)
  other arithmetic  8.19 us (5%)
  matrix products  7.16 us (5%)
  starting transfers between devices  3.65 us (2%)
    all_gather x1, waiting for transfers between devices, shards(): whole = lax.all_gather(own_columns, 'col', axis=3, tiled=True)  83.5 us
    all_to_all x1, blocking collectives, shards(): lax.all_to_all(leaving, 'row', split_axis=3, concat_axis=3, tiled=True)  17.8 us
    all_to_all x1, waiting for transfers between devices, shards(): lax.all_to_all(outgoing, 'row', split_axis=1, concat_axis=1, tiled=True)  12.7 us
    dot_general x2, matrix products, right_piece(): product = jnp.dot(flat, weight, preferred_element_type=jnp.float32)  4.15 us
    all_to_all x1, starting transfers between devices, shards(): lax.all_to_all(outgoing, 'row', split_axis=1, concat_axis=1, tiled=True)  3.65 us
  transfers between devices with their start and end apart: 2, of which 2 were waited for; matrix products, arithmetic and copies ran while one was open for 3% of the time, Pallas kernels for 0%

commit v1 on v0

--- a/solution.py
+++ b/solution.py
@@ -1,7 +1,264 @@
+import functools
+
 import jax
 import jax.numpy as jnp
 from jax import lax
+from jax.experimental import pallas as pl
+from jax.experimental.pallas import tpu as pltpu
 from jax.sharding import PartitionSpec as P
+
+MESH = pl.DeviceIdType.MESH
+BRANCH_ORDER = (1, 0, 3, 2)
+CHUNKS = {1: 1, 0: 1, 3: 1, 2: 2}
+MAX_CHUNKS = 2
+TAIL_CHUNKS = 2
+LANES = 128
+
+
+def kernel(rows, cols, stem_ref, branch_ref, out_ref,
+           stem_v, whole, hcat, hneg, step_v, moved, leave, fin,
+           up_send, up_recv, dn_send, dn_recv, own_sem, stem_sem,
+           mid_send, mid_recv, mid_own, fin_send, fin_recv, fin_own):
+    order = stem_ref.shape[1]
+    width = branch_ref.shape[3]
+    share = order // rows
+    me = lax.axis_index("row")
+    z = lax.axis_index("col")
+    has_up = z < cols - 1
+    has_dn = z > 0
+
+    stem_copy = pltpu.make_async_copy(stem_ref, stem_v, stem_sem)
+    stem_copy.start()
+    own_copies = {}
+    own_lanes = pl.ds(pl.multiple_of(z * width, width), width)
+    for b in BRANCH_ORDER:
+        own_copies[b] = pltpu.make_async_copy(branch_ref.at[b], whole.at[b, :, :, own_lanes], own_sem.at[b])
+        own_copies[b].start()
+
+    barrier = pltpu.get_barrier_semaphore()
+    for d in range(1, rows):
+        pl.semaphore_signal(barrier, inc=1, device_id={"row": lax.rem(me + d, rows)}, device_id_type=MESH)
+
+    @pl.when(has_up)
+    def _():
+        pl.semaphore_signal(barrier, inc=1, device_id={"col": z + 1}, device_id_type=MESH)
+
+    @pl.when(has_dn)
+    def _():
+        pl.semaphore_signal(barrier, inc=1, device_id={"col": z - 1}, device_id_type=MESH)
+
+    pl.semaphore_wait(barrier, rows - 1 + has_up.astype(jnp.int32) + has_dn.astype(jnp.int32))
+
+    def block_at(b, ch, origin):
+        step = order // CHUNKS[b]
+        lanes = pl.ds(pl.multiple_of(origin * width, width), width)
+        return whole.at[b, :, ch * step:(ch + 1) * step, lanes]
+
+    def own_at(b, ch):
+        step = order // CHUNKS[b]
+        return branch_ref.at[b, :, ch * step:(ch + 1) * step, :]
+
+    def up_copy(b, ch, k, origin, own=False):
+        return pltpu.make_async_remote_copy(
+            src_ref=own_at(b, ch) if own else block_at(b, ch, origin), dst_ref=block_at(b, ch, origin),
+            send_sem=up_send.at[b, ch, k], recv_sem=up_recv.at[b, ch, k],
+            device_id={"col": z + 1}, device_id_type=MESH)
+
+    def dn_copy(b, ch, k, origin, own=False):
+        return pltpu.make_async_remote_copy(
+            src_ref=own_at(b, ch) if own else block_at(b, ch, origin), dst_ref=block_at(b, ch, origin),
+            send_sem=dn_send.at[b, ch, k], recv_sem=dn_recv.at[b, ch, k],
+            device_id={"col": z - 1}, device_id_type=MESH)
+
+    def send_own(b):
+        for ch in range(CHUNKS[b]):
+            @pl.when(has_up)
+            def _():
+                up_copy(b, ch, 0, z, own=True).start()
+
+            @pl.when(has_dn)
+            def _():
+                dn_copy(b, ch, 0, z, own=True).start()
+
+    def collect(b, ch):
+        for k in range(cols - 1):
+            @pl.when(z - 1 - k >= 0)
+            def _():
+                up_copy(b, ch, k, z - 1 - k).wait_recv()
+
+                @pl.when(has_up)
+                def _():
+                    up_copy(b, ch, k + 1, z - 1 - k).start()
+
+            @pl.when(z + 1 + k <= cols - 1)
+            def _():
+                dn_copy(b, ch, k, z + 1 + k).wait_recv()
+
+                @pl.when(has_dn)
+                def _():
+                    dn_copy(b, ch, k + 1, z + 1 + k).start()
+
+    def nt(a, w):
+        return lax.dot_general(a, w, (((1,), (1,)), ((), ())), preferred_element_type=jnp.float32)
+
+    def nn(w, a):
+        return lax.dot_general(w, a, (((1,), (0,)), ((), ())), preferred_element_type=jnp.float32)
+
+    tile = order // 2
+
+    def right(b, source):
+        def body(m, _):
+            at = pl.ds(pl.multiple_of(m * tile, tile), tile)
+            real_in, imag_in = source(at)
+            real = nt(real_in, whole[b, 0]) - nt(imag_in, whole[b, 1])
+            real = real.astype(jnp.bfloat16)
+            hcat[at, :order] = real
+            hneg[at, order:] = real
+            imag = nt(real_in, whole[b, 1]) + nt(imag_in, whole[b, 0])
+            imag = imag.astype(jnp.bfloat16)
+            hcat[at, order:] = imag
+            hneg[at, :order] = -imag
+            return 0
+
+        lax.fori_loop(0, order // tile, body, 0)
+
+    def left(b, at):
+        return nn(whole[b, 0, at, :], hcat[...]) + nn(whole[b, 1, at, :], hneg[...])
+
+    send_own(1)
+    send_own(0)
+    stem_copy.wait()
+    own_copies[1].wait()
+    collect(1, 0)
+    send_own(3)
+    right(1, lambda at: (stem_v[0, at, :], stem_v[1, at, :]))
+    own_copies[0].wait()
+    collect(0, 0)
+    send_own(2)
+
+    def left_first(m, _):
+        at = pl.ds(pl.multiple_of(m * tile, tile), tile)
+        step_v[at, :] = left(0, at).astype(jnp.bfloat16)
+        return 0
+
+    lax.fori_loop(0, order // tile, left_first, 0)
+
+    def rows_of(p):
+        return pl.ds(pl.multiple_of(p * share, share), share)
+
+    def mid_copy(d, to, at):
+        return pltpu.make_async_remote_copy(
+            src_ref=step_v.at[rows_of(to), :], dst_ref=moved.at[rows_of(at), :],
+            send_sem=mid_send.at[d - 1], recv_sem=mid_recv.at[d - 1],
+            device_id={"row": to}, device_id_type=MESH)
+
+    for d in range(1, rows):
+        mid_copy(d, lax.rem(me + d, rows), me).start()
+    mid_own_copy = pltpu.make_async_copy(step_v.at[rows_of(me), :], moved.at[rows_of(me), :], mid_own)
+    mid_own_copy.start()
+
+    own_copies[3].wait()
+    collect(3, 0)
+    for d in range(1, rows):
+        mid_copy(d, lax.rem(me + d, rows), lax.rem(me + rows - d, rows)).wait_recv()
+    mid_own_copy.wait()
+    right(3, lambda at: (moved[at, :order], moved[at, order:]))
+
+    own_copies[2].wait()
+    tail = order // TAIL_CHUNKS
+    lane = lax.broadcasted_iota(jnp.int32, (tail, LANES), 1)
+    low = lane < share
+
+    def fin_copy(t, d, to, at):
+        span = slice(t * tail, (t + 1) * tail)
+        return pltpu.make_async_remote_copy(
+            src_ref=leave.at[to, span, :], dst_ref=fin.at[at, span, :],
+            send_sem=fin_send.at[t, d - 1], recv_sem=fin_recv.at[t, d - 1],
+            device_id={"row": to}, device_id_type=MESH)
+
+    def fin_own_copy(t):
+        span = slice(t * tail, (t + 1) * tail)
+        return pltpu.make_async_copy(leave.at[me, span, :], fin.at[me, span, :], fin_own.at[t])
+
+    per = CHUNKS[2] // TAIL_CHUNKS
+    for t in range(TAIL_CHUNKS):
+        for ch in range(t * per, (t + 1) * per):
+            collect(2, ch)
+        at = pl.ds(t * tail, tail)
+        made = left(2, at)
+        for pair in range(rows // 2):
+            real = made[:, pair * LANES:(pair + 1) * LANES]
+            imag = made[:, order + pair * LANES:order + (pair + 1) * LANES]
+            first = jnp.where(low, real, pltpu.roll(imag, share, 1))
+            second = jnp.where(low, pltpu.roll(real, share, 1), imag)
+            leave[2 * pair, at, :] = first.astype(jnp.bfloat16)
+            leave[2 * pair + 1, at, :] = second.astype(jnp.bfloat16)
+        for d in range(1, rows):
+            fin_copy(t, d, lax.rem(me + d, rows), me).start()
+        fin_own_copy(t).start()
+
+    for t in range(TAIL_CHUNKS):
+        at = pl.ds(t * tail, tail)
+        fin_own_copy(t).wait()
+        for d in range(1, rows):
+            fin_copy(t, d, lax.rem(me + d, rows), lax.rem(me + rows - d, rows)).wait_recv()
+        for pair in range(rows // 2):
+            first = fin[2 * pair, at, :].astype(jnp.float32)
+            second = fin[2 * pair + 1, at, :].astype(jnp.float32)
+            lanes = slice(pair * LANES, (pair + 1) * LANES)
+            real = jnp.where(low, first, pltpu.roll(second, share, 1))
+            imag = jnp.where(low, pltpu.roll(first, share, 1), second)
+            out_ref[0, at, lanes] = real.astype(jnp.bfloat16)
+            out_ref[1, at, lanes] = imag.astype(jnp.bfloat16)
+
+    for b in BRANCH_ORDER:
+        for ch in range(CHUNKS[b]):
+            for k in range(cols - 1):
+                @pl.when((z - k >= 0) & has_up)
+                def _():
+                    up_copy(b, ch, k, z - k).wait_send()
+
+                @pl.when((z + k <= cols - 1) & has_dn)
+                def _():
+                    dn_copy(b, ch, k, z + k).wait_send()
+    for d in range(1, rows):
+        mid_copy(d, lax.rem(me + d, rows), me).wait_send()
+        for t in range(TAIL_CHUNKS):
+            fin_copy(t, d, lax.rem(me + d, rows), me).wait_send()
+
+
+def fused(stem, branch):
+    order = stem.shape[3]
+    rows = lax.axis_size("row")
+    cols = lax.axis_size("col")
+    split = jnp.transpose(stem[0, 0, 0], (1, 0, 2))
+    bf16 = jnp.bfloat16
+    dma = pltpu.SemaphoreType.DMA
+    hops = max(cols - 1, 1)
+    result = pl.pallas_call(
+        functools.partial(kernel, rows, cols),
+        out_shape=jax.ShapeDtypeStruct((2, order, order), bf16),
+        in_specs=[pl.BlockSpec(memory_space=pl.ANY)] * 2,
+        out_specs=pl.BlockSpec(memory_space=pltpu.VMEM),
+        scratch_shapes=[
+            pltpu.VMEM((2, order, order), bf16),
+            pltpu.VMEM((4, 2, order, order), bf16),
+            pltpu.VMEM((order, 2 * order), bf16),
+            pltpu.VMEM((order, 2 * order), bf16),
+            pltpu.VMEM((order, 2 * order), bf16),
+            pltpu.VMEM((order, 2 * order), bf16),
+            pltpu.VMEM((rows, order, LANES), bf16),
+            pltpu.VMEM((rows, order, LANES), bf16),
+            dma((4, MAX_CHUNKS, hops)), dma((4, MAX_CHUNKS, hops)),
+            dma((4, MAX_CHUNKS, hops)), dma((4, MAX_CHUNKS, hops)),
+            dma((4,)), dma,
+            dma((rows - 1,)), dma((rows - 1,)), dma,
+            dma((TAIL_CHUNKS, rows - 1)), dma((TAIL_CHUNKS, rows - 1)), dma((TAIL_CHUNKS,)),
+        ],
+        compiler_params=pltpu.CompilerParams(
+            collective_id=0, has_side_effects=True, vmem_limit_bytes=48 * 1024 * 1024),
+    )(split, branch[0])
+    return jnp.transpose(result, (1, 0, 2))[None, None, None]
 
 
 def right_piece(block, piece):
@@ -31,32 +288,30 @@
     return jnp.stack([product[:, :rows_out, :], product[:, rows_out:, :]], axis=2)
 
 
-def shards(stem, branch):
+def plain(stem, branch):
     slab_count = stem.shape[2]
     order_size = stem.shape[3]
     row_count = lax.axis_size("row")
     share = order_size // row_count
-    own_columns = branch[0]
-    whole = lax.all_gather(own_columns, "col", axis=3, tiled=True)
-
-    def apply_right(block, build_id):
-        return right_piece(block, whole[build_id])
-
-    def apply_left(block, build_id):
-        return left_piece(block, whole[build_id])
-
-    block = stem[0, 0]
-    half_first = apply_right(block, 1).astype(jnp.bfloat16)
-    step_first = apply_left(half_first, 0).astype(jnp.bfloat16)
+    whole = lax.all_gather(branch[0], "col", axis=3, tiled=True)
+    half_first = right_piece(stem[0, 0], whole[1]).astype(jnp.bfloat16)
+    step_first = left_piece(half_first, whole[0]).astype(jnp.bfloat16)
     outgoing = step_first.reshape(slab_count, row_count, share, 2, order_size)
     moved = lax.all_to_all(outgoing, "row", split_axis=1, concat_axis=1, tiled=True)
-    items = moved.shape[0]
-    flat = moved.reshape(items, order_size, 2, order_size)
-    half_second = apply_right(flat, 3).astype(jnp.bfloat16)
-    step_second = apply_left(half_second, 2).astype(jnp.bfloat16)
+    flat = moved.reshape(moved.shape[0], order_size, 2, order_size)
+    half_second = right_piece(flat, whole[3]).astype(jnp.bfloat16)
+    step_second = left_piece(half_second, whole[2]).astype(jnp.bfloat16)
     leaving = step_second.reshape(slab_count, order_size, 2, row_count, share)
     arrived = lax.all_to_all(leaving, "row", split_axis=3, concat_axis=3, tiled=True)
     return arrived.reshape(1, 1, slab_count, order_size, 2, order_size)
+
+
+def shards(stem, branch):
+    order = stem.shape[3]
+    rows = lax.axis_size("row")
+    fits = (stem.shape[2] == 1 and branch.shape[4] % LANES == 0
+            and order % (2 * LANES) == 0 and 2 * (order // rows) == LANES)
+    return fused(stem, branch) if fits else plain(stem, branch)
 
 
 def solution(mesh):

time: 158 us -> 87.8 us (0.56)
  waiting for transfers between devices: 96.9 us -> 0 us
  Pallas kernels: 0 us -> 84 us
  blocking collectives: 17.8 us -> 0 us
  between operations: 13.5 us -> 0.01 us
  other arithmetic: 8.19 us -> 0 us
  matrix products: 7.16 us -> 0 us
  local copies, waits for them, and re-layouts: 10.5 us -> 3.59 us
  starting transfers between devices: 3.65 us -> 0 us
    pallas_call x0 -> x1, Pallas kernels: none -> 84 us  [fused(): pl.pallas_call(functools.partial(kernel, rows, cols), out_shape=jax.Shape...]
    all_gather x1 -> x0, waiting for transfers between devices: 83.5 us -> none  [shards(): whole = lax.all_gather(own_columns, 'col', axis=3, tiled=True)]
    all_to_all x1 -> x0, blocking collectives: 17.8 us -> none  [shards(): lax.all_to_all(leaving, 'row', split_axis=3, concat_axis=3, tiled=True)]
    all_to_all x1 -> x0, waiting for transfers between devices: 12.7 us -> none  [shards(): lax.all_to_all(outgoing, 'row', split_axis=1, concat_axis=1, tiled=True)]
    dot_general x6 -> x0, matrix products: 7.16 us -> none  [the longest x2 4.15 us: right_piece(): product = jnp.dot(flat, weight, preferred_element_type=jnp.float32)]
    neg x2 -> x0, other arithmetic: 4.28 us -> none  [the longest x1 2.22 us: left_piece(): weight_imag = jnp.concatenate([-imag_w, real_w], axis=0)]
    all_to_all x1 -> x0, starting transfers between devices: 3.65 us -> none  [shards(): lax.all_to_all(outgoing, 'row', split_axis=1, concat_axis=1, tiled=True)]
    slice x4 -> x0, local copies, waits for them, and re-layouts: 3.21 us -> none  [the longest x3 2.2 us: left_piece(): product[:, :rows_out, :]]
  transfers between devices with their start and end apart: 2 -> 0, of which waited for: 2 -> 0; matrix products, arithmetic and copies ran while one was open for 3% -> 0% of each run, Pallas kernels for 0% -> 0%
where the time goes in v1:
time: 87.8 us; the launch traced here: 87.6 us
  Pallas kernels  84 us (96%)
  local copies, waits for them, and re-layouts  3.59 us (4%)
    pallas_call x1, Pallas kernels, fused(): pl.pallas_call(functools.partial(kernel, rows, cols), out_shape=jax.Shape...  84 us
    broadcast_in_dim x1, local copies, waits for them, and re-layouts, fused(): return jnp.transpose(result, (1, 0, 2))[None, None, None]  2.05 us

profile of v1, /device:TPU:0, one launch (start us, length us, event | category | flops | bytes accessed | tf_op | source)
XLA Modules:
  0.0 87.6 jit_solution(6834135392282367679)
XLA Ops:
  0.0 0.0 copy-start
  0.0 1.5 %copy.6 = bf16[1,1,1,512,2,512]{5,3,4,2,1,0:T(8,128)(2,1)S(1)} copy(bf16[1,1,1,512,2,512]{5,4,3,2,1,0:T(2,128)(2,1)} %param.2) | data formatting | bytes 2097152 | tf_op args[0]
  1.5 0.1 copy-done
  1.5 84.0 %shard_map.28 = bf16[2,512,512]{2,1,0:T(8,128)(2,1)S(1)} custom-call(bf16[2,512,512]{2,1,0:T(8,128)(2,1)S(1)} %bitcast.10, bf16[4,2,512,128]{3,2,1,0:T(8,128)(2,1)S(1)} %bitcast.11), custom_call_target="tpu_custom_call" | custom-call | tf_op jit(solution)/shard_map/pallas_call | solution.py:238
  85.5 2.0 %copy.4 = bf16[1,1,1,512,2,512]{5,4,3,2,1,0:T(2,128)(2,1)} copy(bf16[1,1,1,512,2,512]{5,3,4,2,1,0:T(8,128)(2,1)S(1)} %bitcast.9) | data formatting | bytes 2097152 | tf_op jit(solution)/shard_map/broadcast_in_dim | solution.py:261
Async XLA Ops:
  0.0 1.5 %copy-start = (bf16[1,4,2,512,128]{4,3,2,1,0:T(8,128)(2,1)S(1)}, bf16[1,4,2,512,128]{4,3,2,1,0:T(8,128)(2,1)}, u32[]{:S(2)}) copy-start(bf16[1,4,2,512,128]{4,3,2,1,0:T(8,128)(2,1)} %param.3) | copy-start | bytes 3145732

commit v2 on v1

v2 whole, which is shorter than its diff:
```python
import functools

import jax
import jax.numpy as jnp
from jax import lax
from jax.experimental import pallas as pl
from jax.experimental.pallas import tpu as pltpu
from jax.sharding import PartitionSpec as P

MESH = pl.DeviceIdType.MESH
BRANCH_ORDER = (1, 0, 3, 2)
CHUNKS = {1: 1, 0: 1, 3: 1, 2: 4}
MAX_CHUNKS = 4
TAIL_CHUNKS = 4
LANES = 128


def kernel(rows, cols, stem_ref, branch_ref, out_ref,
           stem_v, whole, hcat, hneg, step_v, moved, leave, fin,
           up_send, up_recv, dn_send, dn_recv, own_sem, stem_sem, guest_send, guest_recv,
           mid_send, mid_recv, mid_own, fin_send, fin_recv, fin_own):
    order = stem_ref.shape[1]
    width = branch_ref.shape[3]
    share = order // rows
    me = lax.axis_index("row")
    z = lax.axis_index("col")
    odd = lax.rem(me, 2) == 1
    partner = z + 1 - 2 * lax.rem(z, 2)
    end = (z == 0) | (z == cols - 1)
    lends = end & odd
    hosts = jnp.logical_not(end) & odd
    works = jnp.logical_not(lends)
    units = works.astype(jnp.int32) + hosts.astype(jnp.int32)
    has_up = z < cols - 1
    has_dn = z > 0
    feeds_up = has_up & jnp.logical_not((z == cols - 2) & odd)
    feeds_dn = has_dn & jnp.logical_not((z == 1) & odd)

    stem_copy = pltpu.make_async_copy(stem_ref, stem_v.at[0], stem_sem)
    stem_copy.start()
    own_copies = {}
    own_lanes = pl.ds(pl.multiple_of(z * width, width), width)
    for b in BRANCH_ORDER:
        own_copies[b] = pltpu.make_async_copy(branch_ref.at[b], whole.at[b, :, :, own_lanes], own_sem.at[b])
        own_copies[b].start()

    barrier = pltpu.get_barrier_semaphore()
    for d in range(1, rows):
        peer = lax.rem(me + d, rows)
        pl.semaphore_signal(barrier, inc=1, device_id={"row": peer}, device_id_type=MESH)
        pl.semaphore_signal(barrier, inc=1, device_id={"row": peer, "col": partner}, device_id_type=MESH)

    @pl.when(has_up)
    def _():
        pl.semaphore_signal(barrier, inc=1, device_id={"col": z + 1}, device_id_type=MESH)

    @pl.when(has_dn)
    def _():
        pl.semaphore_signal(barrier, inc=1, device_id={"col": z - 1}, device_id_type=MESH)

    pl.semaphore_wait(barrier, 2 * (rows - 1) + has_up.astype(jnp.int32) + has_dn.astype(jnp.int32))

    def block_at(b, ch, origin):
        step = order // CHUNKS[b]
        lanes = pl.ds(pl.multiple_of(origin * width, width), width)
        return whole.at[b, :, ch * step:(ch + 1) * step, lanes]

    def own_at(b, ch):
        step = order // CHUNKS[b]
        return branch_ref.at[b, :, ch * step:(ch + 1) * step, :]

    def up_copy(b, ch, k, origin, own=False):
        return pltpu.make_async_remote_copy(
            src_ref=own_at(b, ch) if own else block_at(b, ch, origin), dst_ref=block_at(b, ch, origin),
            send_sem=up_send.at[b, ch, k], recv_sem=up_recv.at[b, ch, k],
            device_id={"col": z + 1}, device_id_type=MESH)

    def dn_copy(b, ch, k, origin, own=False):
        return pltpu.make_async_remote_copy(
            src_ref=own_at(b, ch) if own else block_at(b, ch, origin), dst_ref=block_at(b, ch, origin),
            send_sem=dn_send.at[b, ch, k], recv_sem=dn_recv.at[b, ch, k],
            device_id={"col": z - 1}, device_id_type=MESH)

    def send_own(b):
        for ch in range(CHUNKS[b]):
            @pl.when(feeds_up)
            def _():
                up_copy(b, ch, 0, z, own=True).start()

            @pl.when(feeds_dn)
            def _():
                dn_copy(b, ch, 0, z, own=True).start()

    def collect(b, ch):
        for k in range(cols - 1):
            @pl.when((z - 1 - k >= 0) & works)
            def _():
                up_copy(b, ch, k, z - 1 - k).wait_recv()
                if k + 1 < cols - 1:
                    @pl.when(feeds_up)
                    def _():
                        up_copy(b, ch, k + 1, z - 1 - k).start()

            @pl.when((z + 1 + k <= cols - 1) & works)
            def _():
                dn_copy(b, ch, k, z + 1 + k).wait_recv()
                if k + 1 < cols - 1:
                    @pl.when(feeds_dn)
                    def _():
                        dn_copy(b, ch, k + 1, z + 1 + k).start()

    def nt(a, w):
        return lax.dot_general(a, w, (((1,), (1,)), ((), ())), preferred_element_type=jnp.float32)

    def nn(w, a):
        return lax.dot_general(w, a, (((1,), (0,)), ((), ())), preferred_element_type=jnp.float32)

    halves = 2
    tile = order // halves

    def over_units(make):
        def body(i, _):
            m = lax.rem(i, halves)
            make(i // halves, pl.ds(pl.multiple_of(m * tile, tile), tile))
            return 0

        lax.fori_loop(0, units * halves, body, 0)

    def right(b, source):
        def make(u, at):
            real_in, imag_in = source(u, at)
            real = nt(real_in, whole[b, 0]) - nt(imag_in, whole[b, 1])
            real = real.astype(jnp.bfloat16)
            hcat[u, at, :order] = real
            hneg[u, at, order:] = real
            imag = nt(real_in, whole[b, 1]) + nt(imag_in, whole[b, 0])
            imag = imag.astype(jnp.bfloat16)
            hcat[u, at, order:] = imag
            hneg[u, at, :order] = -imag

        over_units(make)

    def left(b, u, at):
        return nn(whole[b, 0, at, :], hcat[u]) + nn(whole[b, 1, at, :], hneg[u])

    guest_copy = pltpu.make_async_remote_copy(
        src_ref=stem_ref, dst_ref=stem_v.at[1], send_sem=guest_send, recv_sem=guest_recv,
        device_id={"col": partner}, device_id_type=MESH)

    send_own(1)

    @pl.when(lends)
    def _():
        guest_copy.start()

    send_own(0)
    stem_copy.wait()
    own_copies[1].wait()
    collect(1, 0)
    send_own(3)

    @pl.when(hosts)
    def _():
        guest_copy.wait_recv()

    right(1, lambda u, at: (stem_v[u, 0, at, :], stem_v[u, 1, at, :]))
    own_copies[0].wait()
    collect(0, 0)
    send_own(2)

    def left_first(u, at):
        step_v[u, at, :] = left(0, u, at).astype(jnp.bfloat16)

    over_units(left_first)

    def rows_of(p):
        return pl.ds(pl.multiple_of(p * share, share), share)

    def active(u):
        return works if u == 0 else hosts

    def mid_copy(u, d):
        to = lax.rem(me + d, rows)
        q = z if u == 0 else partner
        lent = ((q == 0) | (q == cols - 1)) & (lax.rem(to, 2) == 1)
        slot = lent.astype(jnp.int32)
        home = z + slot * (partner - z) if u == 0 else partner + slot * (z - partner)
        return pltpu.make_async_remote_copy(
            src_ref=step_v.at[u, rows_of(to), :], dst_ref=moved.at[slot, rows_of(me), :],
            send_sem=mid_send.at[u, d - 1], recv_sem=mid_recv.at[slot, d - 1],
            device_id={"row": to, "col": home}, device_id_type=MESH)

    def mid_arrival(u, d):
        origin = lax.rem(me + rows - d, rows)
        return pltpu.make_async_remote_copy(
            src_ref=step_v.at[u, rows_of(origin), :], dst_ref=moved.at[u, rows_of(origin), :],
            send_sem=mid_send.at[u, d - 1], recv_sem=mid_recv.at[u, d - 1],
            device_id={"row": origin}, device_id_type=MESH)

    def mid_own_copy(u):
        return pltpu.make_async_copy(step_v.at[u, rows_of(me), :], moved.at[u, rows_of(me), :], mid_own.at[u])

    for u in (1, 0):
        @pl.when(active(u))
        def _():
            for d in range(1, rows):
                mid_copy(u, d).start()
            mid_own_copy(u).start()

    own_copies[3].wait()
    collect(3, 0)
    for u in (0, 1):
        @pl.when(active(u))
        def _():
            for d in range(1, rows):
                mid_arrival(u, d).wait_recv()
            mid_own_copy(u).wait()

    right(3, lambda u, at: (moved[u, at, :order], moved[u, at, order:]))

    own_copies[2].wait()
    tail = order // TAIL_CHUNKS
    lane = lax.broadcasted_iota(jnp.int32, (tail, LANES), 1)
    low = lane < share

    def fin_copy(u, t, d):
        span = slice(t * tail, (t + 1) * tail)
        to = lax.rem(me + d, rows)
        return pltpu.make_async_remote_copy(
            src_ref=leave.at[u, to, span, :], dst_ref=fin.at[me, span, :],
            send_sem=fin_send.at[u, t, d], recv_sem=fin_recv.at[t, d],
            device_id={"row": to, "col": z if u == 0 else partner}, device_id_type=MESH)

    def fin_arrival(t, d):
        span = slice(t * tail, (t + 1) * tail)
        origin = lax.rem(me + rows - d, rows)
        return pltpu.make_async_remote_copy(
            src_ref=leave.at[0, origin, span, :], dst_ref=fin.at[origin, span, :],
            send_sem=fin_send.at[0, t, d], recv_sem=fin_recv.at[t, d],
            device_id={"row": origin, "col": partner}, device_id_type=MESH)

    def fin_own_copy(t):
        span = slice(t * tail, (t + 1) * tail)
        return pltpu.make_async_copy(leave.at[0, me, span, :], fin.at[me, span, :], fin_own.at[t])

    for t in range(TAIL_CHUNKS):
        collect(2, t)
        at = pl.ds(t * tail, tail)
        for u in (1, 0):
            @pl.when(active(u))
            def _():
                made = left(2, u, at)
                for pair in range(rows // 2):
                    real = made[:, pair * LANES:(pair + 1) * LANES]
                    imag = made[:, order + pair * LANES:order + (pair + 1) * LANES]
                    first = jnp.where(low, real, pltpu.roll(imag, share, 1))
                    second = jnp.where(low, pltpu.roll(real, share, 1), imag)
                    leave[u, 2 * pair, at, :] = first.astype(jnp.bfloat16)
                    leave[u, 2 * pair + 1, at, :] = second.astype(jnp.bfloat16)
                for d in range(u == 0, rows):
                    fin_copy(u, t, d).start()
                if u == 0:
                    fin_own_copy(t).start()

    for t in range(TAIL_CHUNKS):
        at = pl.ds(t * tail, tail)

        @pl.when(works)
        def _():
            fin_own_copy(t).wait()

        @pl.when(lends)
        def _():
            fin_arrival(t, 0).wait_recv()

        for d in range(1, rows):
            fin_arrival(t, d).wait_recv()
        for pair in range(rows // 2):
            first = fin[2 * pair, at, :].astype(jnp.float32)
            second = fin[2 * pair + 1, at, :].astype(jnp.float32)
            lanes = slice(pair * LANES, (pair + 1) * LANES)
            real = jnp.where(low, first, pltpu.roll(second, share, 1))
            imag = jnp.where(low, pltpu.roll(first, share, 1), second)
            out_ref[0, at, lanes] = real.astype(jnp.bfloat16)
            out_ref[1, at, lanes] = imag.astype(jnp.bfloat16)

    for b in BRANCH_ORDER:
        for ch in range(CHUNKS[b]):
            for k in range(cols - 1):
                @pl.when((z - k >= 0) & feeds_up)
                def _():
                    up_copy(b, ch, k, z - k).wait_send()

                @pl.when((z + k <= cols - 1) & feeds_dn)
                def _():
                    dn_copy(b, ch, k, z + k).wait_send()

    @pl.when(lends)
    def _():
        guest_copy.wait_send()

    for u in (0, 1):
        @pl.when(active(u))
        def _():
            for d in range(1, rows):
                mid_copy(u, d).wait_send()
            for t in range(TAIL_CHUNKS):
                for d in range(u == 0, rows):
                    fin_copy(u, t, d).wait_send()


def fused(stem, branch):
    order = stem.shape[3]
    rows = lax.axis_size("row")
    cols = lax.axis_size("col")
    split = jnp.transpose(stem[0, 0, 0], (1, 0, 2))
    bf16 = jnp.bfloat16
    dma = pltpu.SemaphoreType.DMA
    hops = dma((4, MAX_CHUNKS, cols - 1))
    result = pl.pallas_call(
        functools.partial(kernel, rows, cols),
        out_shape=jax.ShapeDtypeStruct((2, order, order), bf16),
        in_specs=[pl.BlockSpec(memory_space=pl.ANY)] * 2,
        out_specs=pl.BlockSpec(memory_space=pltpu.VMEM),
        scratch_shapes=[
            pltpu.VMEM((2, 2, order, order), bf16),
            pltpu.VMEM((4, 2, order, order), bf16),
            pltpu.VMEM((2, order, 2 * order), bf16),
            pltpu.VMEM((2, order, 2 * order), bf16),
            pltpu.VMEM((2, order, 2 * order), bf16),
            pltpu.VMEM((2, order, 2 * order), bf16),
            pltpu.VMEM((2, rows, order, LANES), bf16),
            pltpu.VMEM((rows, order, LANES), bf16),
            hops, hops, hops, hops,
            dma((4,)), dma, dma, dma,
            dma((2, rows - 1)), dma((2, rows - 1)), dma((2,)),
            dma((2, TAIL_CHUNKS, rows)), dma((TAIL_CHUNKS, rows)), dma((TAIL_CHUNKS,)),
        ],
        compiler_params=pltpu.CompilerParams(
            collective_id=0, has_side_effects=True, vmem_limit_bytes=48 * 1024 * 1024),
    )(split, branch[0])
    return jnp.transpose(result, (1, 0, 2))[None, None, None]


def right_piece(block, piece):
    width = piece.shape[2]
    items = block.shape[0]
    order_size = block.shape[1]
    flat = block.reshape(items * order_size, 2 * width)
    real_t = piece[0].T
    imag_t = piece[1].T
    weight = jnp.block([[real_t, imag_t], [-imag_t, real_t]])
    product = jnp.dot(flat, weight, preferred_element_type=jnp.float32)
    return product.reshape(items, order_size, 2, order_size)


def left_piece(block, piece):
    rows_out = piece.shape[1]
    real_in = block[:, :, 0, :]
    imag_in = block[:, :, 1, :]
    real_w = piece[0]
    imag_w = piece[1]
    weight_real = jnp.concatenate([real_w, imag_w], axis=0)
    weight_imag = jnp.concatenate([-imag_w, real_w], axis=0)
    product = jnp.einsum("xi,eij->exj", weight_real, real_in, preferred_element_type=jnp.float32)
    product = product + jnp.einsum(
        "xi,eij->exj", weight_imag, imag_in, preferred_element_type=jnp.float32
    )
    return jnp.stack([product[:, :rows_out, :], product[:, rows_out:, :]], axis=2)


def plain(stem, branch):
    slab_count = stem.shape[2]
    order_size = stem.shape[3]
    row_count = lax.axis_size("row")
    share = order_size // row_count
    whole = lax.all_gather(branch[0], "col", axis=3, tiled=True)
    half_first = right_piece(stem[0, 0], whole[1]).astype(jnp.bfloat16)
    step_first = left_piece(half_first, whole[0]).astype(jnp.bfloat16)
    outgoing = step_first.reshape(slab_count, row_count, share, 2, order_size)
    moved = lax.all_to_all(outgoing, "row", split_axis=1, concat_axis=1, tiled=True)
    flat = moved.reshape(moved.shape[0], order_size, 2, order_size)
    half_second = right_piece(flat, whole[3]).astype(jnp.bfloat16)
    step_second = left_piece(half_second, whole[2]).astype(jnp.bfloat16)
    leaving = step_second.reshape(slab_count, order_size, 2, row_count, share)
    arrived = lax.all_to_all(leaving, "row", split_axis=3, concat_axis=3, tiled=True)
    return arrived.reshape(1, 1, slab_count, order_size, 2, order_size)


def shards(stem, branch):
    order = stem.shape[3]
    rows = lax.axis_size("row")
    fits = (stem.shape[2] == 1 and lax.axis_size("col") == 4 and branch.shape[4] % LANES == 0
            and order % (2 * LANES) == 0 and 2 * (order // rows) == LANES)
    return fused(stem, branch) if fits else plain(stem, branch)


def solution(mesh):
    placed = (P("row", "col", None, None, None, None), P("row", None, None, None, "col"))
    return jax.shard_map(
        shards,
        mesh=mesh,
        in_specs=placed,
        out_specs=P("row", "col", None, None, None, None),
        check_vma=False,
    )
```

time: 87.8 us -> 88.8 us (1.011)
  Pallas kernels: 84 us -> 85.1 us
    pallas_call x1, Pallas kernels: 84 us -> 85.1 us  [fused(): pl.pallas_call(functools.partial(kernel, rows, cols), out_shape=jax.Shape...]
where the time goes in v2:
time: 88.8 us; the launch traced here: 88.7 us
  Pallas kernels  85.1 us (96%)
  local copies, waits for them, and re-layouts  3.59 us (4%)
    pallas_call x1, Pallas kernels, fused(): pl.pallas_call(functools.partial(kernel, rows, cols), out_shape=jax.Shape...  85.1 us
    broadcast_in_dim x1, local copies, waits for them, and re-layouts, fused(): return jnp.transpose(result, (1, 0, 2))[None, None, None]  2.05 us

profile of v2, /device:TPU:0, one launch (start us, length us, event | category | flops | bytes accessed | tf_op | source)
XLA Modules:
  0.0 88.7 jit_solution(10850214866259197426)
XLA Ops:
  0.0 0.0 copy-start
  0.0 1.5 %copy.6 = bf16[1,1,1,512,2,512]{5,3,4,2,1,0:T(8,128)(2,1)S(1)} copy(bf16[1,1,1,512,2,512]{5,4,3,2,1,0:T(2,128)(2,1)} %param.2) | data formatting | bytes 2097152 | tf_op args[0]
  1.5 0.1 copy-done
  1.5 85.1 %shard_map.28 = bf16[2,512,512]{2,1,0:T(8,128)(2,1)S(1)} custom-call(bf16[2,512,512]{2,1,0:T(8,128)(2,1)S(1)} %bitcast.10, bf16[4,2,512,128]{3,2,1,0:T(8,128)(2,1)S(1)} %bitcast.11), custom_call_target="tpu_custom_call" | custom-call | tf_op jit(solution)/shard_map/pallas_call | solution.py:320
  86.6 2.0 %copy.4 = bf16[1,1,1,512,2,512]{5,4,3,2,1,0:T(2,128)(2,1)} copy(bf16[1,1,1,512,2,512]{5,3,4,2,1,0:T(8,128)(2,1)S(1)} %bitcast.9) | data formatting | bytes 2097152 | tf_op jit(solution)/shard_map/broadcast_in_dim | solution.py:342
Async XLA Ops:
  0.0 1.5 %copy-start = (bf16[1,4,2,512,128]{4,3,2,1,0:T(8,128)(2,1)S(1)}, bf16[1,4,2,512,128]{4,3,2,1,0:T(8,128)(2,1)}, u32[]{:S(2)}) copy-start(bf16[1,4,2,512,128]{4,3,2,1,0:T(8,128)(2,1)} %param.3) | copy-start | bytes 3145732

commit v3 on v2

--- a/solution.py
+++ b/solution.py
@@ -81,33 +81,42 @@
             send_sem=dn_send.at[b, ch, k], recv_sem=dn_recv.at[b, ch, k],
             device_id={"col": z - 1}, device_id_type=MESH)
 
-    def send_own(b):
+    def send_own(b, who):
         for ch in range(CHUNKS[b]):
-            @pl.when(feeds_up)
+            @pl.when(feeds_up & who)
             def _():
                 up_copy(b, ch, 0, z, own=True).start()
 
-            @pl.when(feeds_dn)
+            @pl.when(feeds_dn & who)
             def _():
                 dn_copy(b, ch, 0, z, own=True).start()
 
-    def collect(b, ch):
-        for k in range(cols - 1):
-            @pl.when((z - 1 - k >= 0) & works)
+    def sent_own(b, who):
+        for ch in range(CHUNKS[b]):
+            @pl.when(feeds_up & who)
             def _():
-                up_copy(b, ch, k, z - 1 - k).wait_recv()
-                if k + 1 < cols - 1:
-                    @pl.when(feeds_up)
-                    def _():
-                        up_copy(b, ch, k + 1, z - 1 - k).start()
-
-            @pl.when((z + 1 + k <= cols - 1) & works)
+                up_copy(b, ch, 0, z, own=True).wait_send()
+
+            @pl.when(feeds_dn & who)
             def _():
-                dn_copy(b, ch, k, z + 1 + k).wait_recv()
-                if k + 1 < cols - 1:
-                    @pl.when(feeds_dn)
-                    def _():
-                        dn_copy(b, ch, k + 1, z + 1 + k).start()
+                dn_copy(b, ch, 0, z, own=True).wait_send()
+
+    def collect_hop(b, ch, k):
+        @pl.when((z - 1 - k >= 0) & works)
+        def _():
+            up_copy(b, ch, k, z - 1 - k).wait_recv()
+            if k + 1 < cols - 1:
+                @pl.when(feeds_up)
+                def _():
+                    up_copy(b, ch, k + 1, z - 1 - k).start()
+
+        @pl.when((z + 1 + k <= cols - 1) & works)
+        def _():
+            dn_copy(b, ch, k, z + 1 + k).wait_recv()
+            if k + 1 < cols - 1:
+                @pl.when(feeds_dn)
+                def _():
+                    dn_copy(b, ch, k + 1, z + 1 + k).start()
 
     def nt(a, w):
         return lax.dot_general(a, w, (((1,), (1,)), ((), ())), preferred_element_type=jnp.float32)
@@ -147,26 +156,48 @@
         src_ref=stem_ref, dst_ref=stem_v.at[1], send_sem=guest_send, recv_sem=guest_recv,
         device_id={"col": partner}, device_id_type=MESH)
 
-    send_own(1)
+    middle = jnp.logical_not(end)
+    keeps = end & works
+    always = z >= 0
+    send_own(1, always)
+    send_own(0, always)
+
+    sent_own(1, lends)
 
     @pl.when(lends)
     def _():
         guest_copy.start()
 
-    send_own(0)
+    sent_own(0, lends)
+
+    @pl.when(lends)
+    def _():
+        guest_copy.wait_send()
+
+    send_own(3, lends)
+    sent_own(3, lends)
+    send_own(2, lends)
+    sent_own(2, lends)
+
     stem_copy.wait()
     own_copies[1].wait()
-    collect(1, 0)
-    send_own(3)
+    own_copies[0].wait()
+    collect_hop(1, 0, 0)
+    send_own(3, middle)
+    collect_hop(0, 0, 0)
+    collect_hop(1, 0, 1)
+    send_own(2, middle)
+    send_own(3, keeps)
+    collect_hop(1, 0, 2)
+    collect_hop(0, 0, 1)
+    send_own(2, keeps)
+    collect_hop(0, 0, 2)
 
     @pl.when(hosts)
     def _():
         guest_copy.wait_recv()
 
     right(1, lambda u, at: (stem_v[u, 0, at, :], stem_v[u, 1, at, :]))
-    own_copies[0].wait()
-    collect(0, 0)
-    send_own(2)
 
     def left_first(u, at):
         step_v[u, at, :] = left(0, u, at).astype(jnp.bfloat16)
@@ -208,7 +239,11 @@
             mid_own_copy(u).start()
 
     own_copies[3].wait()
-    collect(3, 0)
+    collect_hop(3, 0, 0)
+    for t in range(TAIL_CHUNKS):
+        collect_hop(2, t, 0)
+    collect_hop(3, 0, 1)
+    collect_hop(3, 0, 2)
     for u in (0, 1):
         @pl.when(active(u))
         def _():
@@ -244,7 +279,8 @@
         return pltpu.make_async_copy(leave.at[0, me, span, :], fin.at[me, span, :], fin_own.at[t])
 
     for t in range(TAIL_CHUNKS):
-        collect(2, t)
+        collect_hop(2, t, 1)
+        collect_hop(2, t, 2)
         at = pl.ds(t * tail, tail)
         for u in (1, 0):
             @pl.when(active(u))
@@ -287,17 +323,13 @@
     for b in BRANCH_ORDER:
         for ch in range(CHUNKS[b]):
             for k in range(cols - 1):
-                @pl.when((z - k >= 0) & feeds_up)
+                @pl.when((z - k >= 0) & feeds_up & works)
                 def _():
                     up_copy(b, ch, k, z - k).wait_send()
 
-                @pl.when((z + k <= cols - 1) & feeds_dn)
+                @pl.when((z + k <= cols - 1) & feeds_dn & works)
                 def _():
                     dn_copy(b, ch, k, z + k).wait_send()
-
-    @pl.when(lends)
-    def _():
-        guest_copy.wait_send()
 
     for u in (0, 1):
         @pl.when(active(u))

time: 88.8 us -> 83.7 us (0.943)
  Pallas kernels: 85.1 us -> 80 us
    pallas_call x1, Pallas kernels: 85.1 us -> 80 us  [fused(): pl.pallas_call(functools.partial(kernel, rows, cols), out_shape=jax.Shape...]
where the time goes in v3:
time: 83.7 us; the launch traced here: 83.6 us
  Pallas kernels  80 us (96%)
  local copies, waits for them, and re-layouts  3.59 us (4%)
    pallas_call x1, Pallas kernels, fused(): pl.pallas_call(functools.partial(kernel, rows, cols), out_shape=jax.Shape...  80 us
    broadcast_in_dim x1, local copies, waits for them, and re-layouts, fused(): return jnp.transpose(result, (1, 0, 2))[None, None, None]  2.05 us

profile of v3, /device:TPU:0, one launch (start us, length us, event | category | flops | bytes accessed | tf_op | source)
XLA Modules:
  0.0 83.6 jit_solution(329471848998075186)
XLA Ops:
  0.0 0.0 copy-start
  0.0 1.5 %copy.6 = bf16[1,1,1,512,2,512]{5,3,4,2,1,0:T(8,128)(2,1)S(1)} copy(bf16[1,1,1,512,2,512]{5,4,3,2,1,0:T(2,128)(2,1)} %param.2) | data formatting | bytes 2097152 | tf_op args[0]
  1.5 0.1 copy-done
  1.5 80.0 %shard_map.28 = bf16[2,512,512]{2,1,0:T(8,128)(2,1)S(1)} custom-call(bf16[2,512,512]{2,1,0:T(8,128)(2,1)S(1)} %bitcast.10, bf16[4,2,512,128]{3,2,1,0:T(8,128)(2,1)S(1)} %bitcast.11), custom_call_target="tpu_custom_call" | custom-call | tf_op jit(solution)/shard_map/pallas_call | solution.py:352
  81.5 2.0 %copy.4 = bf16[1,1,1,512,2,512]{5,4,3,2,1,0:T(2,128)(2,1)} copy(bf16[1,1,1,512,2,512]{5,3,4,2,1,0:T(8,128)(2,1)S(1)} %bitcast.9) | data formatting | bytes 2097152 | tf_op jit(solution)/shard_map/broadcast_in_dim | solution.py:374
Async XLA Ops:
  0.0 1.5 %copy-start = (bf16[1,4,2,512,128]{4,3,2,1,0:T(8,128)(2,1)S(1)}, bf16[1,4,2,512,128]{4,3,2,1,0:T(8,128)(2,1)}, u32[]{:S(2)}) copy-start(bf16[1,4,2,512,128]{4,3,2,1,0:T(8,128)(2,1)} %param.3) | copy-start | bytes 3145732
